TPU v7x, 256 devices: a whole 4x4x8 slice. The times are simulated.
256 devices in a mesh: replica: 8 (over z_lo, x), fsdp: 32 (over y, z_hi, core).
Axes of the slice: x: 4, y: 4, z: 8 (z_hi: 4, z_lo: 2; z = z_hi * 2 + z_lo), core: 2. Of those that a mesh axis runs over, the one named last changes fastest.
Arguments:
- tokens: bfloat16 [8, 8192, 8192], P('replica', 'fsdp'), may hold values from -6 to 6
- queries: bfloat16 [8, 8192, 4096], P('replica', 'fsdp'), may hold values from -480 to 480
- segments: int32 [8, 32, 256], P('replica', 'fsdp'), may hold values from 0 to 7, never falling along the last dimension, each value on 1 to 128 neighbouring positions
- local_weights: bfloat16 [8, 8192, 1024], P('replica', 'fsdp'), may hold values from -6 to 6
- global_params: float32 [8192, 1024], P('fsdp'), may hold values from -6 to 6
- momentum: float32 [8192, 1024], P('fsdp'), may hold values from -6 to 6
Outputs:
- attended: bfloat16 [8, 8192, 4096], P('replica', 'fsdp')
- new_params: float32 [8192, 1024], P('fsdp')
- new_momentum: float32 [8192, 1024], P('fsdp')
Inputs may be any that keep to these rules, and one draw needn't show every extreme that they name: `segments`: document numbers never fall along a sequence; each document has 1 to 128 positions and one has exactly 128.
All inputs are finite; a program needn't handle non-finite values.
Results may differ from a plain program's by a relative error of at most 0.012.
The roundings to bfloat16 on the way count: a program that leaves them out, or rounds other values in their place, can miss the bound.
Values may be sent and summed in bfloat16 or wider, within the bound.
A program may use at most 128 MiB of HBM per device.

v0:
```python
import jax
import jax.numpy as jnp
from jax import lax
from jax.sharding import PartitionSpec as P

HD = 128
HEADS_KV = 4
Q_GROUP = 8
QH = 32


def nesterov(params, moment, outer_grad):
    fresh_moment = 0.9 * moment + outer_grad
    fresh_params = params - 0.7 * (outer_grad + 0.9 * fresh_moment)
    return (fresh_params, fresh_moment)


def shards(tokens, queries, segments, local_weights, global_params, momentum):
    features = tokens[0]
    rows_dev = features.shape[0]
    width = features.shape[1]
    projected = jnp.dot(
        features,
        lax.all_gather(local_weights, "fsdp", axis=1, tiled=True)[0],
        preferred_element_type=jnp.float32,
    )
    pairs = (projected * width ** (-0.5)).astype(jnp.bfloat16)
    keys = pairs[:, : HEADS_KV * HD].reshape(rows_dev, HEADS_KV, HD)
    values = pairs[:, HEADS_KV * HD :].reshape(rows_dev, HEADS_KV, HD)
    query_heads = queries[0].reshape(rows_dev, HEADS_KV, Q_GROUP, HD)
    scores = jnp.einsum(
        "thgd,shd->hgts", query_heads, keys, preferred_element_type=jnp.float32
    ) * HD ** (-0.5)
    doc_ids = segments[0, 0]
    position = lax.iota(jnp.int32, rows_dev)
    allowed = (doc_ids[:, None] == doc_ids[None, :]) & (position[None, :] <= position[:, None])
    scores = jnp.where(allowed, scores, -jnp.inf)
    row_max = jnp.max(scores, axis=-1, keepdims=True)
    weights = jnp.exp(scores - row_max)
    probs = (weights / jnp.sum(weights, axis=-1, keepdims=True)).astype(jnp.bfloat16)
    mixed = jnp.einsum("hgts,shd->thgd", probs, values, preferred_element_type=jnp.float32)
    attended = mixed.reshape(1, rows_dev, QH * HD).astype(jnp.bfloat16)
    term = global_params - local_weights[0].astype(jnp.float32)
    replicas = lax.axis_size("replica")
    total = lax.psum(term, "replica")
    new_params, new_momentum = nesterov(global_params, momentum, total / replicas)
    return (attended, new_params, new_momentum)


def solution(mesh):
    placed = (
        P("replica", "fsdp", None),
        P("replica", "fsdp", None),
        P("replica", "fsdp", None),
        P("replica", "fsdp", None),
        P("fsdp", None),
        P("fsdp", None),
    )
    return jax.shard_map(
        shards,
        mesh=mesh,
        in_specs=placed,
        out_specs=(P("replica", "fsdp", None), P("fsdp", None), P("fsdp", None)),
        check_vma=False,
    )
```

profile of v0, /device:TPU:72, one launch (start us, length us, event | category | flops | bytes accessed | tf_op | source)
XLA Modules:
  0.0 186.5 jit_solution(6796579293504106778)
XLA Ops:
  8.0 0.0 copy-start
  8.0 0.0 copy-start.1
  8.0 0.0 all-reduce.2.cloned.1.call-start
  8.1 2.6 %convert_subtract_fusion = f32[256,1024]{1,0:T(8,128)} fusion(f32[256,1024]{1,0:T(8,128)} %param.10, bf16[1,256,1024]{2,1,0:T(8,128)(2,1)} %param.9), kind=kLoop, calls=%fused_computation.17 | loop fusion | flops 524288 | bytes 2621440 | tf_op jit(solution)/shard_map/sub | solution.py:43
  10.7 0.0 all-reduce.2.cloned.1.call-update
  10.7 0.0 all-gather.2.cloned.1.call-start
  10.7 0.5 all-gather.2.cloned.1.call-update
  11.3 2.1 %copy.20 = bf16[32,8,32,128]{3,2,1,0:T(8,128)(2,1)S(1)} copy(bf16[32,8,32,128]{3,1,2,0:T(8,128)(2,1)} %bitcast.44) | data formatting | bytes 4194304
  13.3 0.0 copy-done.1
  13.3 0.1 fusion.23
  13.5 143.2 %all-reduce.2.cloned.1.call-done = f32[256,1024]{1,0:T(8,128)} async-done(((f32[256,1024]{1,0:T(8,128)}), f32[256,1024]{1,0:T(8,128)}) %all-reduce.2.cloned.1.call-update) | async-done | bytes 1048592 | tf_op jit(solution)/shard_map/psum | solution.py:45
  156.7 0.0 copy-done
  156.7 3.3 %multiply_subtract_fusion = (f32[256,1024]{1,0:T(8,128)}, f32[256,1024]{1,0:T(8,128)}) fusion(f32[256,1024]{1,0:T(8,128)S(1)} %copy-done, f32[256,1024]{1,0:T(8,128)} %all-reduce.2.cloned.1.call-done, f32[256,1024]{1,0:T(8,128)} %param.11), kind=kLoop, calls=%fused_computation.18 | loop fusion | flops 1835008 | bytes 5242880 | tf_op jit(solution)/shard_map/sub | solution.py:14
  160.0 0.0 all-gather.2.cloned.1.call-done
  160.0 11.5 %fusion.17 = bf16[256,1024]{1,0:T(8,128)(2,1)S(1)} fusion(bf16[1,8192,1024]{2,1,0:T(8,128)(2,1)} %all-gather.2.cloned.1.call-done, bf16[1,256,8192]{2,1,0:T(8,128)(2,1)} %param.6), kind=kOutput, calls=%fused_computation.16 | convolution fusion | flops 4295491584 | bytes 21495808 | tf_op jit(solution)/shard_map/dot_general | solution.py:22
  171.6 0.1 reshape.33
  171.7 0.1 copy.17
  171.8 1.4 fusion.9
  173.2 2.3 %fusion.27 = (f32[4,8,256]{2,1,0:T(8,128)S(1)}, f32[4,8,256,256]{2,3,1,0:T(8,128)S(1)}) fusion(f32[4,256,256,8]{2,1,3,0:T(8,128)S(1)} %fusion.9, pred[256,256]{0,1:T(8,128)(4,1)S(1)} %fusion.23), kind=kOutput, calls=%fused_computation.26 | output fusion | flops 12583167 | bytes 16875520 | tf_op jit(solution)/shard_map/sub | solution.py:39
  175.4 0.8 fusion.11
  176.2 2.9 %copy.13 = bf16[1,256,4096]{2,1,0:T(8,128)(2,1)} copy(bf16[1,256,4096]{1,2,0:T(8,128)(2,1)S(1)} %bitcast.45) | data formatting | bytes 4194304
  (1 shorter events, 0.0 us)
Async XLA Ops:
  8.0 148.7 %copy-start = (f32[256,1024]{1,0:T(8,128)S(1)}, f32[256,1024]{1,0:T(8,128)}, u32[]{:S(2)}) copy-start(f32[256,1024]{1,0:T(8,128)} %param.10) | copy-start | bytes 3145732
  8.0 5.3 %copy-start.1 = (s32[1,1,256]{2,1,0:T(1,128)S(1)}, s32[1,1,256]{2,1,0:T(1,128)}, u32[]{:S(2)}) copy-start(s32[1,1,256]{2,1,0:T(1,128)} %param.8) | copy-start | bytes 3076
  8.0 148.7 %all-reduce.2.cloned.1.call-start = ((), (), s32[]{:S(2)}) async-start(), calls=%async_computation.1 | async-start | bytes 2097152 | tf_op jit(solution)/shard_map/psum | solution.py:45
  10.7 149.3 %all-gather.2.cloned.1.call-start = ((), (), s32[]{:S(2)}) async-start(), calls=%async_computation | async-start | bytes 17301504 | tf_op jit(solution)/shard_map/all_gather | solution.py:24
Sparse Core Ops, SparseCore 0:
  12.1 144.5 all-reduce.1
Sparse Core Ops, SparseCore 1:
  13.7 122.8 all-gather.1
where the time goes:
time: 187 us
  waiting for transfers between devices  144 us (77%)
  between operations  15.6 us (8%)
  matrix products  13.7 us (7%)
  other arithmetic  8.27 us (4%)
  local copies, waits for them, and re-layouts  5.17 us (3%)
    psum x1, waiting for transfers between devices, shards(): total = lax.psum(term, 'replica')  143 us
    dot_general x1, matrix products, shards(): jnp.dot(features, lax.all_gather(local_weights, 'fsdp', axis=1, tiled=Tru...  11.5 us
    unnamed x6, local copies, waits for them, and re-layouts  4.94 us
  transfers between devices with their start and end apart: 2, of which 1 were waited for; matrix products, arithmetic and copies ran while one was open for 3% of the time, Pallas kernels for 0%

commit v1 on v0

v1 whole, which is shorter than its diff:
```python
import math

import jax
import jax.numpy as jnp
from jax import lax
from jax.experimental import pallas as pl
from jax.experimental.pallas import tpu as pltpu
from jax.sharding import PartitionSpec as P

HD = 128
QH = 32
Q_GROUP = 8
ROWS = 256
WIDTH = 8192
KVW = 1024
BLK = 256
NQ = KVW // BLK
CHIPS = 16
X = 4
PART = ROWS // X
MESH = pl.DeviceIdType.MESH

NODES = (
    (0, 1), (0, -1), (1, 0), (-1, 0), (2, 0),
    (1, 1), (-1, 1), (1, -1), (-1, -1), (0, 2),
    (2, 1), (2, -1), (1, 2), (-1, 2), (2, 2),
)
TREE = {
    (0, 0): ((0, 1), (0, -1), (1, 0), (-1, 0)),
    (0, 1): ((0, 2), (1, 1), (-1, 1)),
    (0, -1): ((1, -1), (-1, -1)),
    (1, 0): ((2, 0),),
    (1, 1): ((1, 2),),
    (-1, 1): ((2, 1),),
    (1, -1): ((2, -1),),
    (-1, -1): ((-1, 2),),
    (-1, 2): ((2, 2),),
}
PARENT = {child: node for node, children in TREE.items() for child in children}
ORDER = (
    -18, -34, -2, -19, -16, -49, -33, -47, -17, -1, 17, -32, -4, 1, 15,
    7, 19, 16, 0, 46, -3, 21, 8, 11, 22, 18, 23, 31, 20, -46,
    28, 38, 3, 32, 33, 13, 2, 5, 24, 29, 26, 9, 6, 25, -31,
    45, 53, -48, 27, 48, 43, 4, 12, 10, 14, 50, 30, 47, 51, 37,
    44, 58, 52, 36, 35, 49, 54, 41, 57, 34, 39, 59, 55, 56, 40,
    42,
)
GROUP = 4
RECEIVES = [code for code in ORDER if code >= 0]
SUM_AT, SPREAD_AT, UPDATE_AT = 10, 36, 52


def kernel(
    tokens, queries, segs, weights, params, moment,
    attended, new_params, new_moment,
    gathered, feats, acc, incoming, qv, bias, probs, keys, mixed,
    raw, partsum, partin, total, gv, mv,
    gsend, grecv, tsend, trecv, xsend, xrecv, zsend, zrecv, bsend, brecv, psend, precv,
    own_sem, feat_sem, q_sem, raw_sem, g_sem, m_sem, o_sem, np_sem, nm_sem,
):
    r = lax.axis_index("replica")
    f = lax.axis_index("fsdp")
    zl, x = r // X, r % X
    y, zh, c = f // 8, (f // 2) % 4, f % 2
    sign = 1 - 2 * c
    other = 1 - c
    sibling = (r, f + 1 - 2 * c)
    zpeer = ((1 - zl) * X + x, f)

    def xpeer(step):
        return (zl * X + (x + step) % X, f)

    def dev(dy, dz):
        return (r, (((y + dy + 4) % 4) * 4 + (zh + dz * sign + 4) % 4) * 2 + c)

    def slot(node):
        return ((y - node[0] + 4) % 4) * 4 + (zh - node[1] * sign + 4) % 4

    own = y * 4 + zh

    own_feats = [
        pltpu.make_async_copy(
            tokens.at[:, pl.ds(pl.multiple_of((2 * o + c) * BLK, BLK), BLK)],
            feats.at[o, pl.ds(pl.multiple_of(c * ROWS, ROWS), ROWS)],
            feat_sem,
        )
        for o in range(CHIPS)
    ]
    own_weights = [
        pltpu.make_async_copy(weights.at[:, pl.ds(q * BLK, BLK)], gathered.at[own, q], own_sem.at[q])
        for q in range(NQ)
    ]
    q_copy = pltpu.make_async_copy(queries, qv, q_sem)
    g_copy = pltpu.make_async_copy(params, gv, g_sem)
    m_copy = pltpu.make_async_copy(moment, mv, m_sem)
    raw_copy = pltpu.make_async_copy(weights.at[pl.ds(pl.multiple_of(x * PART, PART), PART)], raw.at[x], raw_sem)

    barrier = pltpu.get_barrier_semaphore()
    peers = [dev(1, 0), dev(-1, 0), dev(0, 1), dev(0, -1), sibling, zpeer, xpeer(1), xpeer(2), xpeer(3)]
    for peer in peers:
        pl.semaphore_signal(barrier, inc=1, device_id=peer, device_id_type=MESH)
    for copy in own_weights + own_feats:
        copy.start()
    raw_copy.start()
    pl.semaphore_wait(barrier, len(peers))

    def hop(q, child):
        node = PARENT[child]
        at, index = slot(node), NODES.index(child)
        source = weights.at[:, pl.ds(q * BLK, BLK)] if node == (0, 0) else gathered.at[at, q]
        return pltpu.make_async_remote_copy(
            src_ref=source, dst_ref=gathered.at[at, q],
            send_sem=gsend.at[q, index], recv_sem=grecv.at[q, index],
            device_id=dev(*step_of(child)), device_id_type=MESH,
        )

    def step_of(child):
        node = PARENT[child]
        dy, dz = (child[0] - node[0]) % 4, (child[1] - node[1]) % 4
        return (dy - 4 if dy == 3 else dy, dz - 4 if dz == 3 else dz)

    def arrive(q, node):
        at, index = slot(node), NODES.index(node)
        pltpu.make_async_remote_copy(
            src_ref=gathered.at[at, q], dst_ref=gathered.at[at, q],
            send_sem=gsend.at[q, index], recv_sem=grecv.at[q, index],
            device_id=sibling, device_id_type=MESH,
        ).wait_recv()

    def feat_send(o):
        return pltpu.make_async_remote_copy(
            src_ref=tokens.at[:, pl.ds(pl.multiple_of((2 * o + other) * BLK, BLK), BLK)],
            dst_ref=feats.at[o, pl.ds(pl.multiple_of(c * ROWS, ROWS), ROWS)],
            send_sem=tsend, recv_sem=trecv, device_id=sibling, device_id_type=MESH,
        )

    def all_feats(row_core):
        view = feats.at[:, pl.ds(pl.multiple_of(row_core * ROWS, ROWS), ROWS)]
        return pltpu.make_async_remote_copy(
            src_ref=view, dst_ref=view, send_sem=tsend, recv_sem=trecv, device_id=sibling, device_id_type=MESH
        )

    def raw_send(step):
        to = (x + step) % X
        return pltpu.make_async_remote_copy(
            src_ref=weights.at[pl.ds(pl.multiple_of(to * PART, PART), PART)], dst_ref=raw.at[x],
            send_sem=xsend.at[step - 1], recv_sem=xrecv.at[step - 1], device_id=xpeer(step), device_id_type=MESH,
        )

    def raw_arrive(step):
        at = (x - step + X) % X
        pltpu.make_async_remote_copy(
            src_ref=raw.at[at], dst_ref=raw.at[at],
            send_sem=xsend.at[step - 1], recv_sem=xrecv.at[step - 1], device_id=xpeer(step), device_id_type=MESH,
        ).wait_recv()

    z_copy = pltpu.make_async_remote_copy(
        src_ref=partsum, dst_ref=partin, send_sem=zsend, recv_sem=zrecv, device_id=zpeer, device_id_type=MESH
    )

    def spread(step):
        return pltpu.make_async_remote_copy(
            src_ref=total.at[x], dst_ref=total.at[x],
            send_sem=bsend.at[step - 1], recv_sem=brecv.at[step - 1], device_id=xpeer(step), device_id_type=MESH,
        )

    def spread_arrive(step):
        at = (x - step + X) % X
        pltpu.make_async_remote_copy(
            src_ref=total.at[at], dst_ref=total.at[at],
            send_sem=bsend.at[step - 1], recv_sem=brecv.at[step - 1], device_id=xpeer(step), device_id_type=MESH,
        ).wait_recv()

    def exchange(q):
        return pltpu.make_async_remote_copy(
            src_ref=acc.at[q, pl.ds(pl.multiple_of(other * ROWS, ROWS), ROWS)], dst_ref=incoming.at[q],
            send_sem=psend.at[q], recv_sem=precv.at[q], device_id=sibling, device_id_type=MESH,
        )

    def multiply(q, nodes, fresh=False):
        slots = [slot(node) for node in nodes]

        @pl.loop(0, 2)
        def _(half):
            at = pl.ds(pl.multiple_of(half * ROWS, ROWS), ROWS)
            partial = None
            for s in slots:
                term = jnp.dot(feats[s, at, :], gathered[s, q], preferred_element_type=jnp.float32)
                partial = term if partial is None else partial + term
            acc[q, at, :] = partial if fresh else acc[q, at, :] + partial

    def finish_block(q):
        mine = acc[q, pl.ds(pl.multiple_of(c * ROWS, ROWS), ROWS), :]
        return ((mine + incoming[q]) * WIDTH ** (-0.5)).astype(jnp.bfloat16)

    def softmax_heads(start):
        kv = start // Q_GROUP

        @pl.loop(0, 2)
        def _(i):
            h = start + i
            head = qv[:, pl.ds(pl.multiple_of(h * HD, HD), HD)]
            scores = lax.dot_general(
                head, keys[:, kv * HD : (kv + 1) * HD], (((1,), (1,)), ((), ())), preferred_element_type=jnp.float32
            )
            scores = scores * (HD ** (-0.5) * math.log2(math.e)) + bias[...]
            top = jnp.max(scores, axis=1, keepdims=True)
            weight = jnp.exp2(scores - top)
            norm = 1.0 / jnp.sum(weight, axis=1, keepdims=True)
            probs[h] = (weight * norm).astype(jnp.bfloat16)

    def mix(q):
        first = (q - 2) * 2 * Q_GROUP
        block = finish_block(q)
        for j in range(2):
            values = block[:, j * HD : (j + 1) * HD]
            base = first + j * Q_GROUP

            @pl.loop(0, Q_GROUP)
            def _(i):
                h = base + i
                out = jnp.dot(probs[h], values, preferred_element_type=jnp.float32)
                mixed[:, pl.ds(pl.multiple_of(h * HD, HD), HD)] = out.astype(jnp.bfloat16)

        return pltpu.make_async_copy(
            mixed.at[:, pl.ds(first * HD, 2 * Q_GROUP * HD)], attended.at[:, pl.ds(first * HD, 2 * Q_GROUP * HD)],
            o_sem.at[q - 2],
        )

    def sum_raw():
        for step in (1, 2, 3):
            raw_arrive(step)
        raw_copy.wait()
        partsum[...] = (
            raw[0].astype(jnp.float32) + raw[1].astype(jnp.float32) + raw[2].astype(jnp.float32) + raw[3].astype(jnp.float32)
        )
        z_copy.start()

    def spread_total():
        z_copy.wait()
        total[x] = partsum[...] + partin[...]
        for step in (1, 2, 3):
            spread(step).start()

    np_copy = pltpu.make_async_copy(gv, new_params, np_sem)
    nm_copy = pltpu.make_async_copy(mv, new_moment, nm_sem)

    def update():
        for step in (1, 2, 3):
            spread_arrive(step)
        g_copy.wait()
        m_copy.wait()

        @pl.loop(0, X)
        def _(j):
            at = pl.ds(pl.multiple_of(j * PART, PART), PART)
            g = gv[at, :]
            grad = g - total[j] * 0.125
            fresh = 0.9 * mv[at, :] + grad
            mv[at, :] = fresh
            gv[at, :] = g - 0.7 * (grad + 0.9 * fresh)

        np_copy.start()
        nm_copy.start()

    pending = {q: [] for q in range(NQ)}
    left = {q: CHIPS - 1 for q in range(NQ)}
    started = set()
    todo = []
    state = {"ready": False, "queries": False}

    def flush(q):
        if pending[q]:
            multiply(q, pending[q], fresh=q not in started)
            started.add(q)
            pending[q] = []

    outs = []

    def settle(q):
        exchange(q).wait_recv()
        if q < 2:
            keys[:, q * BLK : (q + 1) * BLK] = finish_block(q)
            if not state["queries"]:
                state["queries"] = True
                q_copy.wait()
            todo.extend(range(q * 2 * Q_GROUP, (q + 1) * 2 * Q_GROUP, 2))
        else:
            copy = mix(q)
            copy.start()
            outs.append(copy)

    waiting = []
    done = 0
    opened = False
    for code in ORDER:
        if code < 0:
            q, n = divmod(-code - 1, 15)
            hop(q, NODES[n]).start()
            continue
        if not opened:
            opened = True
            for step in (1, 2, 3):
                raw_send(step).start()
            for o in range(CHIPS):
                feat_send(o).start()
            q_copy.start()
            g_copy.start()
            m_copy.start()
            row = lax.broadcast_in_dim(segs[...], (ROWS, ROWS), (0, 1))
            t_at = lax.broadcasted_iota(jnp.int32, (ROWS, ROWS), 0)
            s_at = lax.broadcasted_iota(jnp.int32, (ROWS, ROWS), 1)
            allowed = (row == row.T) & (s_at <= t_at)
            bias[...] = jnp.where(allowed, 0.0, -1e30)
        q, n = divmod(code, 15)
        arrive(q, NODES[n])
        for child in TREE.get(NODES[n], ()):
            hop(q, child).start()
        done += 1
        pending[q].append(NODES[n])
        left[q] -= 1
        if not state["ready"] and done >= 4:
            state["ready"] = True
            for o in own_weights:
                o.wait()
            view = feats.at[:, pl.ds(pl.multiple_of(c * ROWS, ROWS), ROWS)]
            pltpu.make_async_copy(view, view, feat_sem).wait()
            all_feats(other).wait_recv()
            for qq in range(NQ):
                pending[qq].append((0, 0))
        if state["ready"] and (len(pending[q]) >= GROUP or left[q] == 0):
            flush(q)
        for item in list(waiting):
            if done >= item[0] + 2 and (item[1] < 2 or not todo):
                waiting.remove(item)
                settle(item[1])
        if left[q] == 0:
            exchange(q).start()
            waiting.append((done, q))
        if done == SUM_AT:
            sum_raw()
        if done == SPREAD_AT:
            spread_total()
        if done == UPDATE_AT:
            update()
        remaining = len(RECEIVES) - done
        if todo:
            count = -(-len(todo) // max(1, remaining - 3))
            for start in todo[:count]:
                softmax_heads(start)
            del todo[:count]

    for start in todo:
        softmax_heads(start)
    for _, q in waiting:
        settle(q)

    for q in range(NQ):
        for child in NODES:
            hop(q, child).wait_send()
        exchange(q).wait_send()
    all_feats(other).wait_send()
    for step in (1, 2, 3):
        raw_send(step).wait_send()
        spread(step).wait_send()
    np_copy.wait()
    nm_copy.wait()
    for copy in outs:
        copy.wait()


def shards(tokens, queries, segments, local_weights, global_params, momentum):
    any_space = pl.BlockSpec(memory_space=pl.ANY)
    vmem = pl.BlockSpec(memory_space=pltpu.VMEM)
    dma = pltpu.SemaphoreType.DMA
    attended, new_params, new_momentum = pl.pallas_call(
        kernel,
        out_shape=(
            jax.ShapeDtypeStruct((ROWS, QH * HD), jnp.bfloat16),
            jax.ShapeDtypeStruct((ROWS, KVW), jnp.float32),
            jax.ShapeDtypeStruct((ROWS, KVW), jnp.float32),
        ),
        in_specs=[any_space, any_space, vmem, any_space, any_space, any_space],
        out_specs=(any_space, any_space, any_space),
        scratch_shapes=[
            pltpu.VMEM((CHIPS, NQ, BLK, BLK), jnp.bfloat16),
            pltpu.VMEM((CHIPS, 2 * ROWS, BLK), jnp.bfloat16),
            pltpu.VMEM((NQ, 2 * ROWS, BLK), jnp.float32),
            pltpu.VMEM((NQ, ROWS, BLK), jnp.float32),
            pltpu.VMEM((ROWS, QH * HD), jnp.bfloat16),
            pltpu.VMEM((ROWS, ROWS), jnp.float32),
            pltpu.VMEM((QH, ROWS, ROWS), jnp.bfloat16),
            pltpu.VMEM((ROWS, 2 * BLK), jnp.bfloat16),
            pltpu.VMEM((ROWS, QH * HD), jnp.bfloat16),
            pltpu.VMEM((X, PART, KVW), jnp.bfloat16),
            pltpu.VMEM((PART, KVW), jnp.float32),
            pltpu.VMEM((PART, KVW), jnp.float32),
            pltpu.VMEM((X, PART, KVW), jnp.float32),
            pltpu.VMEM((ROWS, KVW), jnp.float32),
            pltpu.VMEM((ROWS, KVW), jnp.float32),
            dma((NQ, 15)), dma((NQ, 15)), dma, dma, dma((3,)), dma((3,)), dma, dma, dma((3,)), dma((3,)),
            dma((NQ,)), dma((NQ,)),
            dma((NQ,)), dma, dma, dma, dma, dma, dma((2,)), dma, dma,
        ],
        compiler_params=pltpu.CompilerParams(
            collective_id=0, has_side_effects=True, vmem_limit_bytes=56 * 2**20
        ),
        cost_estimate=pl.CostEstimate(flops=6 * 10**9, bytes_accessed=13 * 2**20, transcendentals=2**21),
        name="sync_and_attend",
    )(tokens[0], queries[0], segments[0], local_weights[0], global_params, momentum)
    return (attended[None], new_params, new_momentum)


def solution(mesh):
    placed = (
        P("replica", "fsdp", None),
        P("replica", "fsdp", None),
        P("replica", "fsdp", None),
        P("replica", "fsdp", None),
        P("fsdp", None),
        P("fsdp", None),
    )
    return jax.shard_map(
        shards,
        mesh=mesh,
        in_specs=placed,
        out_specs=(P("replica", "fsdp", None), P("fsdp", None), P("fsdp", None)),
        check_vma=False,
    )
```

time: 187 us -> 97.6 us (0.52)
  the two profiles are of different devices: /device:TPU:72 before, /device:TPU:1 now
where the time goes in v1:
time: 97.6 us; the launch traced here: 97.5 us
  Pallas kernels  91.6 us (94%)
  local copies, waits for them, and re-layouts  5.22 us (5%)
    pallas_call x1, Pallas kernels, shards(): pl.pallas_call(kernel, out_shape=(jax.ShapeDtypeStruct((ROWS, QH * HD), j...  91.6 us
    unnamed x7, local copies, waits for them, and re-layouts  5.22 us

profile of v1, /device:TPU:1, one launch (start us, length us, event | category | flops | bytes accessed | tf_op | source)
XLA Modules:
  0.0 97.5 jit_solution(4865091489782678478)
XLA Ops:
  0.6 91.6 %sync_and_attend.1 = (bf16[256,4096]{1,0:T(8,128)(2,1)}, f32[256,1024]{1,0:T(8,128)}, f32[256,1024]{1,0:T(8,128)}) custom-call(bf16[256,8192]{1,0:T(8,128)(2,1)} %bitcast.6, bf16[256,4096]{1,0:T(8,128)(2,1)} %bitcast.7, s32[1,256]{1,0:T(1,128)} %bitcast.9, bf16[256,1024]{1,0:T(8,128)(2,1)} %bitcast.8, f32[256,1024]{1,0:T(8,128)} %params.1, f32[256,1024]{1,0:T(8,128)} %moment.1), custom_call_target="tpu_custom_call" | custom-call | flops 6000000000 | bytes 13631488 | tf_op jit(solution)/shard_map/sync_and_attend/pallas_call | solution.py:376
  92.2 0.0 copy-start.1
  92.2 0.0 copy-start
  92.2 3.3 %copy.12 = bf16[1,256,4096]{2,1,0:T(8,128)(2,1)} copy(bf16[1,256,4096]{2,1,0:T(8,128)(2,1)} %bitcast.5) | data formatting | bytes 4194304
  95.5 0.0 copy-done.1
  95.5 1.0 copy.13
  96.5 0.0 copy-done
  96.5 1.0 copy.14
Async XLA Ops:
  92.2 3.3 %copy-start.1 = (f32[256,1024]{1,0:T(8,128)S(1)}, f32[256,1024]{1,0:T(8,128)}, u32[]{:S(2)}) copy-start(f32[256,1024]{1,0:T(8,128)} %get-tuple-element.13) | copy-start | bytes 3145732
  92.2 4.3 %copy-start = (f32[256,1024]{1,0:T(8,128)S(1)}, f32[256,1024]{1,0:T(8,128)}, u32[]{:S(2)}) copy-start(f32[256,1024]{1,0:T(8,128)} %get-tuple-element.14) | copy-start | bytes 3145732

commit v2 on v1

--- a/solution.py
+++ b/solution.py
@@ -25,38 +25,33 @@
     (1, 1), (-1, 1), (1, -1), (-1, -1), (0, 2),
     (2, 1), (2, -1), (1, 2), (-1, 2), (2, 2),
 )
-TREE = {
-    (0, 0): ((0, 1), (0, -1), (1, 0), (-1, 0)),
-    (0, 1): ((0, 2), (1, 1), (-1, 1)),
-    (0, -1): ((1, -1), (-1, -1)),
-    (1, 0): ((2, 0),),
-    (1, 1): ((1, 2),),
-    (-1, 1): ((2, 1),),
-    (1, -1): ((2, -1),),
-    (-1, -1): ((-1, 2),),
-    (-1, 2): ((2, 2),),
+PARENTS = {
+    (0, 1): (0, 0), (0, -1): (0, 0), (1, 0): (0, 0), (-1, 0): (0, 0), (2, 0): (1, 0),
+    (1, 1): (0, 1), (-1, 1): (0, 1), (1, -1): (0, -1), (-1, -1): (0, -1), (0, 2): (0, 1),
+    (2, 1): (-1, 1), (2, -1): (1, -1), (1, 2): (1, 1), (-1, 2): (-1, -1), (2, 2): (-1, 2),
 }
-PARENT = {child: node for node, children in TREE.items() for child in children}
+TREES = (PARENTS, PARENTS | {(-1, 2): (0, 2)}, PARENTS, PARENTS | {(1, 2): (0, 2)})
 ORDER = (
-    -18, -34, -2, -19, -16, -49, -33, -47, -17, -1, 17, -32, -4, 1, 15,
-    7, 19, 16, 0, 46, -3, 21, 8, 11, 22, 18, 23, 31, 20, -46,
-    28, 38, 3, 32, 33, 13, 2, 5, 24, 29, 26, 9, 6, 25, -31,
-    45, 53, -48, 27, 48, 43, 4, 12, 10, 14, 50, 30, 47, 51, 37,
-    44, 58, 52, 36, 35, 49, 54, 41, 57, 34, 39, 59, 55, 56, 40,
-    42,
+    -2, -3, -49, -33, -47, -16, -4, -17, 1, -1, -18, 46, 8, -34, 16,
+    15, -32, 17, 0, 21, -46, 33, 13, 100, 32, 52, 25, 24, 19, 7,
+    9, 22, -19, 53, -31, 3, 20, 31, 28, 58, 11, -48, 2, 18, 101,
+    5, 26, 23, 45, 56, 6, 29, 30, 48, 27, 47, 34, 14, 59, 12,
+    38, 51, 54, 37, 36, 10, 35, 4, 39, 102, 43, 50, 55, 40, 57,
+    49, 42, 41, 44,
 )
 GROUP = 4
-RECEIVES = [code for code in ORDER if code >= 0]
-SUM_AT, SPREAD_AT, UPDATE_AT = 10, 36, 52
+RECEIVES = [code for code in ORDER if 0 <= code < 100]
+OUTER = 100
+LATE = RECEIVES[-1] // 15 - 2
 
 
 def kernel(
     tokens, queries, segs, weights, params, moment,
-    attended, new_params, new_moment,
-    gathered, feats, acc, incoming, qv, bias, probs, keys, mixed,
-    raw, partsum, partin, total, gv, mv,
+    mixed, late_probs, late_values, gv, mv,
+    gathered, feats, acc, incoming, qv, bias, probs, keys,
+    raw, partsum, partin, total,
     gsend, grecv, tsend, trecv, xsend, xrecv, zsend, zrecv, bsend, brecv, psend, precv,
-    own_sem, feat_sem, q_sem, raw_sem, g_sem, m_sem, o_sem, np_sem, nm_sem,
+    own_sem, feat_sem, q_sem, raw_sem, g_sem, m_sem,
 ):
     r = lax.axis_index("replica")
     f = lax.axis_index("fsdp")
@@ -105,17 +100,17 @@
     pl.semaphore_wait(barrier, len(peers))
 
     def hop(q, child):
-        node = PARENT[child]
+        node = TREES[q][child]
         at, index = slot(node), NODES.index(child)
         source = weights.at[:, pl.ds(q * BLK, BLK)] if node == (0, 0) else gathered.at[at, q]
         return pltpu.make_async_remote_copy(
             src_ref=source, dst_ref=gathered.at[at, q],
             send_sem=gsend.at[q, index], recv_sem=grecv.at[q, index],
-            device_id=dev(*step_of(child)), device_id_type=MESH,
-        )
-
-    def step_of(child):
-        node = PARENT[child]
+            device_id=dev(*step_of(q, child)), device_id_type=MESH,
+        )
+
+    def step_of(q, child):
+        node = TREES[q][child]
         dy, dz = (child[0] - node[0]) % 4, (child[1] - node[1]) % 4
         return (dy - 4 if dy == 3 else dy, dz - 4 if dz == 3 else dz)
 
@@ -207,25 +202,19 @@
             top = jnp.max(scores, axis=1, keepdims=True)
             weight = jnp.exp2(scores - top)
             norm = 1.0 / jnp.sum(weight, axis=1, keepdims=True)
-            probs[h] = (weight * norm).astype(jnp.bfloat16)
+            target = late_probs if start // (2 * Q_GROUP) == LATE else probs
+            target[lax.rem(h, 2 * Q_GROUP)] = (weight * norm).astype(jnp.bfloat16)
 
     def mix(q):
-        first = (q - 2) * 2 * Q_GROUP
         block = finish_block(q)
         for j in range(2):
             values = block[:, j * HD : (j + 1) * HD]
-            base = first + j * Q_GROUP
 
             @pl.loop(0, Q_GROUP)
             def _(i):
-                h = base + i
+                h = j * Q_GROUP + i
                 out = jnp.dot(probs[h], values, preferred_element_type=jnp.float32)
                 mixed[:, pl.ds(pl.multiple_of(h * HD, HD), HD)] = out.astype(jnp.bfloat16)
-
-        return pltpu.make_async_copy(
-            mixed.at[:, pl.ds(first * HD, 2 * Q_GROUP * HD)], attended.at[:, pl.ds(first * HD, 2 * Q_GROUP * HD)],
-            o_sem.at[q - 2],
-        )
 
     def sum_raw():
         for step in (1, 2, 3):
@@ -241,9 +230,6 @@
         total[x] = partsum[...] + partin[...]
         for step in (1, 2, 3):
             spread(step).start()
-
-    np_copy = pltpu.make_async_copy(gv, new_params, np_sem)
-    nm_copy = pltpu.make_async_copy(mv, new_moment, nm_sem)
 
     def update():
         for step in (1, 2, 3):
@@ -260,9 +246,6 @@
             mv[at, :] = fresh
             gv[at, :] = g - 0.7 * (grad + 0.9 * fresh)
 
-        np_copy.start()
-        nm_copy.start()
-
     pending = {q: [] for q in range(NQ)}
     left = {q: CHIPS - 1 for q in range(NQ)}
     started = set()
@@ -274,8 +257,6 @@
             multiply(q, pending[q], fresh=q not in started)
             started.add(q)
             pending[q] = []
-
-    outs = []
 
     def settle(q):
         exchange(q).wait_recv()
@@ -285,10 +266,10 @@
                 state["queries"] = True
                 q_copy.wait()
             todo.extend(range(q * 2 * Q_GROUP, (q + 1) * 2 * Q_GROUP, 2))
+        elif q - 2 == LATE:
+            late_values[...] = finish_block(q)
         else:
-            copy = mix(q)
-            copy.start()
-            outs.append(copy)
+            mix(q)
 
     waiting = []
     done = 0
@@ -297,6 +278,9 @@
         if code < 0:
             q, n = divmod(-code - 1, 15)
             hop(q, NODES[n]).start()
+            continue
+        if code >= OUTER:
+            (sum_raw, spread_total, update)[code - OUTER]()
             continue
         if not opened:
             opened = True
@@ -314,8 +298,9 @@
             bias[...] = jnp.where(allowed, 0.0, -1e30)
         q, n = divmod(code, 15)
         arrive(q, NODES[n])
-        for child in TREE.get(NODES[n], ()):
-            hop(q, child).start()
+        for child in NODES:
+            if TREES[q][child] == NODES[n]:
+                hop(q, child).start()
         done += 1
         pending[q].append(NODES[n])
         left[q] -= 1
@@ -337,12 +322,6 @@
         if left[q] == 0:
             exchange(q).start()
             waiting.append((done, q))
-        if done == SUM_AT:
-            sum_raw()
-        if done == SPREAD_AT:
-            spread_total()
-        if done == UPDATE_AT:
-            update()
         remaining = len(RECEIVES) - done
         if todo:
             count = -(-len(todo) // max(1, remaining - 3))
@@ -363,25 +342,51 @@
     for step in (1, 2, 3):
         raw_send(step).wait_send()
         spread(step).wait_send()
-    np_copy.wait()
-    nm_copy.wait()
-    for copy in outs:
+
+
+def finish_kernel(
+    mixed, late_probs, late_values, gv, mv, attended, new_params, new_moment, late_mixed, early_sem, late_sem, p_sem, m_sem
+):
+    half = 2 * Q_GROUP * HD
+    piece = Q_GROUP * HD
+    early = pltpu.make_async_copy(mixed, attended.at[:, pl.ds((1 - LATE) * half, half)], early_sem)
+    copies = [early, pltpu.make_async_copy(gv, new_params, p_sem), pltpu.make_async_copy(mv, new_moment, m_sem)]
+    for copy in copies:
+        copy.start()
+    for j in range(2):
+        values = late_values[:, j * HD : (j + 1) * HD]
+        for i in range(Q_GROUP):
+            h = j * Q_GROUP + i
+            out = jnp.dot(late_probs[h], values, preferred_element_type=jnp.float32)
+            late_mixed[:, h * HD : (h + 1) * HD] = out.astype(jnp.bfloat16)
+        copy = pltpu.make_async_copy(
+            late_mixed.at[:, pl.ds(j * piece, piece)],
+            attended.at[:, pl.ds(LATE * half + j * piece, piece)],
+            late_sem.at[j],
+        )
+        copy.start()
+        copies.append(copy)
+    for copy in copies:
         copy.wait()
 
 
 def shards(tokens, queries, segments, local_weights, global_params, momentum):
+    hbm = pl.BlockSpec(memory_space=pltpu.HBM)
     any_space = pl.BlockSpec(memory_space=pl.ANY)
     vmem = pl.BlockSpec(memory_space=pltpu.VMEM)
     dma = pltpu.SemaphoreType.DMA
-    attended, new_params, new_momentum = pl.pallas_call(
+    half = 2 * Q_GROUP
+    kept = pl.pallas_call(
         kernel,
         out_shape=(
-            jax.ShapeDtypeStruct((ROWS, QH * HD), jnp.bfloat16),
-            jax.ShapeDtypeStruct((ROWS, KVW), jnp.float32),
-            jax.ShapeDtypeStruct((ROWS, KVW), jnp.float32),
+            pltpu.VMEM((ROWS, half * HD), jnp.bfloat16),
+            pltpu.VMEM((half, ROWS, ROWS), jnp.bfloat16),
+            pltpu.VMEM((ROWS, BLK), jnp.bfloat16),
+            pltpu.VMEM((ROWS, KVW), jnp.float32),
+            pltpu.VMEM((ROWS, KVW), jnp.float32),
         ),
-        in_specs=[any_space, any_space, vmem, any_space, any_space, any_space],
-        out_specs=(any_space, any_space, any_space),
+        in_specs=[hbm, hbm, vmem, hbm, hbm, hbm],
+        out_specs=(vmem,) * 5,
         scratch_shapes=[
             pltpu.VMEM((CHIPS, NQ, BLK, BLK), jnp.bfloat16),
             pltpu.VMEM((CHIPS, 2 * ROWS, BLK), jnp.bfloat16),
@@ -389,25 +394,35 @@
             pltpu.VMEM((NQ, ROWS, BLK), jnp.float32),
             pltpu.VMEM((ROWS, QH * HD), jnp.bfloat16),
             pltpu.VMEM((ROWS, ROWS), jnp.float32),
-            pltpu.VMEM((QH, ROWS, ROWS), jnp.bfloat16),
+            pltpu.VMEM((half, ROWS, ROWS), jnp.bfloat16),
             pltpu.VMEM((ROWS, 2 * BLK), jnp.bfloat16),
-            pltpu.VMEM((ROWS, QH * HD), jnp.bfloat16),
             pltpu.VMEM((X, PART, KVW), jnp.bfloat16),
             pltpu.VMEM((PART, KVW), jnp.float32),
             pltpu.VMEM((PART, KVW), jnp.float32),
             pltpu.VMEM((X, PART, KVW), jnp.float32),
-            pltpu.VMEM((ROWS, KVW), jnp.float32),
-            pltpu.VMEM((ROWS, KVW), jnp.float32),
             dma((NQ, 15)), dma((NQ, 15)), dma, dma, dma((3,)), dma((3,)), dma, dma, dma((3,)), dma((3,)),
             dma((NQ,)), dma((NQ,)),
-            dma((NQ,)), dma, dma, dma, dma, dma, dma((2,)), dma, dma,
+            dma((NQ,)), dma, dma, dma, dma, dma,
         ],
         compiler_params=pltpu.CompilerParams(
-            collective_id=0, has_side_effects=True, vmem_limit_bytes=56 * 2**20
+            collective_id=0, has_side_effects=True, vmem_limit_bytes=57 * 2**20
         ),
         cost_estimate=pl.CostEstimate(flops=6 * 10**9, bytes_accessed=13 * 2**20, transcendentals=2**21),
         name="sync_and_attend",
     )(tokens[0], queries[0], segments[0], local_weights[0], global_params, momentum)
+    attended, new_params, new_momentum = pl.pallas_call(
+        finish_kernel,
+        out_shape=(
+            jax.ShapeDtypeStruct((ROWS, QH * HD), jnp.bfloat16),
+            jax.ShapeDtypeStruct((ROWS, KVW), jnp.float32),
+            jax.ShapeDtypeStruct((ROWS, KVW), jnp.float32),
+        ),
+        in_specs=[vmem] * 5,
+        out_specs=(any_space,) * 3,
+        scratch_shapes=[pltpu.VMEM((ROWS, half * HD), jnp.bfloat16), dma, dma((2,)), dma, dma],
+        compiler_params=pltpu.CompilerParams(vmem_limit_bytes=16 * 2**20),
+        name="finish",
+    )(*kept)
     return (attended[None], new_params, new_momentum)
 
 

time: 97.6 us -> 85.7 us (0.88)
  Pallas kernels: 91.6 us -> 84.9 us
  local copies, waits for them, and re-layouts: 5.22 us -> 0 us
    pallas_call x1 -> x2, Pallas kernels: 91.6 us -> 84.9 us  [the longest x1 82.9 us: shards(): pl.pallas_call(kernel, out_shape=(pltpu.VMEM((ROWS, half * HD), jnp.bfloa...]
    unnamed x7 -> x0, local copies, waits for them, and re-layouts: 5.22 us -> none
where the time goes in v2:
time: 85.7 us; the launch traced here: 85.6 us
  Pallas kernels  84.9 us (99%)
    pallas_call x1, Pallas kernels, shards(): pl.pallas_call(kernel, out_shape=(pltpu.VMEM((ROWS, half * HD), jnp.bfloa...  82.9 us
    pallas_call x1, Pallas kernels, shards(): pl.pallas_call(finish_kernel, out_shape=(jax.ShapeDtypeStruct((ROWS, QH *...  2.06 us

profile of v2, /device:TPU:1, one launch (start us, length us, event | category | flops | bytes accessed | tf_op | source)
XLA Modules:
  0.0 85.6 jit_solution(8779744587505820643)
XLA Ops:
  0.6 82.9 %sync_and_attend.1 = (bf16[256,2048]{1,0:T(8,128)(2,1)S(1)}, bf16[16,256,256]{2,1,0:T(8,128)(2,1)S(1)}, bf16[256,256]{1,0:T(8,128)(2,1)S(1)}, f32[256,1024]{1,0:T(8,128)S(1)}, f32[256,1024]{1,0:T(8,128)S(1)}) custom-call(bf16[256,8192]{1,0:T(8,128)(2,1)} %bitcast.5, bf16[256,4096]{1,0:T(8,128)(2,1)} %bitcast.6, s32[1,256]{1,0:T(1,128)} %bitcast.9, ...), custom_call_target="tpu_custom_call" | custom-call | flops 6000000000 | bytes 13631488 | tf_op jit(solution)/shard_map/sync_and_attend/pallas_call | solution.py:379
  83.5 2.1 %finish.1 = (bf16[256,4096]{1,0:T(8,128)(2,1)}, f32[256,1024]{1,0:T(8,128)}, f32[256,1024]{1,0:T(8,128)}) custom-call(bf16[256,2048]{1,0:T(8,128)(2,1)S(1)} %get-tuple-element.11.mixed, bf16[16,256,256]{2,1,0:T(8,128)(2,1)S(1)} %get-tuple-element.12.late_probs, bf16[256,256]{1,0:T(8,128)(2,1)S(1)} %get-tuple-element.13.late_values, ...), custom_call_target="tpu_custom_call" | custom-call | tf_op jit(solution)/shard_map/finish/pallas_call | solution.py:413

commit v3 on v2

--- a/solution.py
+++ b/solution.py
@@ -42,6 +42,7 @@
 GROUP = 4
 RECEIVES = [code for code in ORDER if 0 <= code < 100]
 OUTER = 100
+TAIL = 55
 LATE = RECEIVES[-1] // 15 - 2
 
 
@@ -173,16 +174,11 @@
         )
 
     def multiply(q, nodes, fresh=False):
-        slots = [slot(node) for node in nodes]
-
-        @pl.loop(0, 2)
-        def _(half):
-            at = pl.ds(pl.multiple_of(half * ROWS, ROWS), ROWS)
-            partial = None
-            for s in slots:
-                term = jnp.dot(feats[s, at, :], gathered[s, q], preferred_element_type=jnp.float32)
-                partial = term if partial is None else partial + term
-            acc[q, at, :] = partial if fresh else acc[q, at, :] + partial
+        partial = None
+        for s in [slot(node) for node in nodes]:
+            term = jnp.dot(feats[s], gathered[s, q], preferred_element_type=jnp.float32)
+            partial = term if partial is None else partial + term
+        acc[q] = partial if fresh else acc[q] + partial
 
     def finish_block(q):
         mine = acc[q, pl.ds(pl.multiple_of(c * ROWS, ROWS), ROWS), :]
@@ -190,31 +186,26 @@
 
     def softmax_heads(start):
         kv = start // Q_GROUP
-
-        @pl.loop(0, 2)
-        def _(i):
-            h = start + i
-            head = qv[:, pl.ds(pl.multiple_of(h * HD, HD), HD)]
+        target = late_probs if start // (2 * Q_GROUP) == LATE else probs
+        for h in range(start, start + 2):
             scores = lax.dot_general(
-                head, keys[:, kv * HD : (kv + 1) * HD], (((1,), (1,)), ((), ())), preferred_element_type=jnp.float32
+                qv[:, h * HD : (h + 1) * HD], keys[:, kv * HD : (kv + 1) * HD],
+                (((1,), (1,)), ((), ())), preferred_element_type=jnp.float32,
             )
             scores = scores * (HD ** (-0.5) * math.log2(math.e)) + bias[...]
             top = jnp.max(scores, axis=1, keepdims=True)
             weight = jnp.exp2(scores - top)
             norm = 1.0 / jnp.sum(weight, axis=1, keepdims=True)
-            target = late_probs if start // (2 * Q_GROUP) == LATE else probs
-            target[lax.rem(h, 2 * Q_GROUP)] = (weight * norm).astype(jnp.bfloat16)
+            target[h % (2 * Q_GROUP)] = (weight * norm).astype(jnp.bfloat16)
 
     def mix(q):
         block = finish_block(q)
         for j in range(2):
             values = block[:, j * HD : (j + 1) * HD]
 
-            @pl.loop(0, Q_GROUP)
-            def _(i):
-                h = j * Q_GROUP + i
+            for h in range(j * Q_GROUP, (j + 1) * Q_GROUP):
                 out = jnp.dot(probs[h], values, preferred_element_type=jnp.float32)
-                mixed[:, pl.ds(pl.multiple_of(h * HD, HD), HD)] = out.astype(jnp.bfloat16)
+                mixed[:, h * HD : (h + 1) * HD] = out.astype(jnp.bfloat16)
 
     def sum_raw():
         for step in (1, 2, 3):
@@ -313,7 +304,7 @@
             all_feats(other).wait_recv()
             for qq in range(NQ):
                 pending[qq].append((0, 0))
-        if state["ready"] and (len(pending[q]) >= GROUP or left[q] == 0):
+        if state["ready"] and (len(pending[q]) >= GROUP or left[q] == 0 or done > TAIL):
             flush(q)
         for item in list(waiting):
             if done >= item[0] + 2 and (item[1] < 2 or not todo):

time: 85.7 us -> 80.9 us (0.944)
  Pallas kernels: 84.9 us -> 80.1 us
    pallas_call x1, Pallas kernels: 82.9 us -> 78.1 us  [shards(): pl.pallas_call(kernel, out_shape=(pltpu.VMEM((ROWS, half * HD), jnp.bfloa...]
where the time goes in v3:
time: 80.9 us; the launch traced here: 80.8 us
  Pallas kernels  80.1 us (99%)
    pallas_call x1, Pallas kernels, shards(): pl.pallas_call(kernel, out_shape=(pltpu.VMEM((ROWS, half * HD), jnp.bfloa...  78.1 us
    pallas_call x1, Pallas kernels, shards(): pl.pallas_call(finish_kernel, out_shape=(jax.ShapeDtypeStruct((ROWS, QH *...  2.06 us

profile of v3, /device:TPU:1, one launch (start us, length us, event | category | flops | bytes accessed | tf_op | source)
XLA Modules:
  0.0 80.8 jit_solution(14042164638989184719)
XLA Ops:
  0.6 78.1 %sync_and_attend.1 = (bf16[256,2048]{1,0:T(8,128)(2,1)S(1)}, bf16[16,256,256]{2,1,0:T(8,128)(2,1)S(1)}, bf16[256,256]{1,0:T(8,128)(2,1)S(1)}, f32[256,1024]{1,0:T(8,128)S(1)}, f32[256,1024]{1,0:T(8,128)S(1)}) custom-call(bf16[256,8192]{1,0:T(8,128)(2,1)} %bitcast.5, bf16[256,4096]{1,0:T(8,128)(2,1)} %bitcast.6, s32[1,256]{1,0:T(1,128)} %bitcast.9, ...), custom_call_target="tpu_custom_call" | custom-call | flops 6000000000 | bytes 13631488 | tf_op jit(solution)/shard_map/sync_and_attend/pallas_call | solution.py:370
  78.7 2.1 %finish.1 = (bf16[256,4096]{1,0:T(8,128)(2,1)}, f32[256,1024]{1,0:T(8,128)}, f32[256,1024]{1,0:T(8,128)}) custom-call(bf16[256,2048]{1,0:T(8,128)(2,1)S(1)} %get-tuple-element.11.mixed, bf16[16,256,256]{2,1,0:T(8,128)(2,1)S(1)} %get-tuple-element.12.late_probs, bf16[256,256]{1,0:T(8,128)(2,1)S(1)} %get-tuple-element.13.late_values, ...), custom_call_target="tpu_custom_call" | custom-call | tf_op jit(solution)/shard_map/finish/pallas_call | solution.py:404

commit v4 on v3

--- a/solution.py
+++ b/solution.py
@@ -30,14 +30,14 @@
     (1, 1): (0, 1), (-1, 1): (0, 1), (1, -1): (0, -1), (-1, -1): (0, -1), (0, 2): (0, 1),
     (2, 1): (-1, 1), (2, -1): (1, -1), (1, 2): (1, 1), (-1, 2): (-1, -1), (2, 2): (-1, 2),
 }
-TREES = (PARENTS, PARENTS | {(-1, 2): (0, 2)}, PARENTS, PARENTS | {(1, 2): (0, 2)})
+TREES = (PARENTS | {(1, 2): (0, 2)}, PARENTS | {(-1, 2): (0, 2)}, PARENTS, PARENTS)
 ORDER = (
-    -2, -3, -49, -33, -47, -16, -4, -17, 1, -1, -18, 46, 8, -34, 16,
-    15, -32, 17, 0, 21, -46, 33, 13, 100, 32, 52, 25, 24, 19, 7,
-    9, 22, -19, 53, -31, 3, 20, 31, 28, 58, 11, -48, 2, 18, 101,
-    5, 26, 23, 45, 56, 6, 29, 30, 48, 27, 47, 34, 14, 59, 12,
-    38, 51, 54, 37, 36, 10, 35, 4, 39, 102, 43, 50, 55, 40, 57,
-    49, 42, 41, 44,
+    -33, -34, -2, -46, -18, -49, -16, -3, -47, -19, 1, -32, -4, 17, 15,
+    -17, -1, 7, 45, 2, 46, 19, 31, 3, 8, -31, 100, 51, 24, 16,
+    -48, 55, 0, 54, 28, 22, 20, 53, 37, 23, 21, 101, 13, 33, 6,
+    48, 4, 5, 38, 30, 9, 27, 29, 47, 26, 52, 25, 18, 14, 58,
+    50, 32, 11, 43, 35, 41, 12, 36, 10, 49, 39, 59, 56, 57, 42,
+    44, 40, 34, 102,
 )
 GROUP = 4
 RECEIVES = [code for code in ORDER if 0 <= code < 100]

time: 80.9 us -> 79.2 us (0.979)
  Pallas kernels: 80.1 us -> 78.5 us
    pallas_call x1, Pallas kernels: 78.1 us -> 76.4 us  [shards(): pl.pallas_call(kernel, out_shape=(pltpu.VMEM((ROWS, half * HD), jnp.bfloa...]
where the time goes in v4:
time: 79.2 us; the launch traced here: 79.1 us
  Pallas kernels  78.5 us (99%)
    pallas_call x1, Pallas kernels, shards(): pl.pallas_call(kernel, out_shape=(pltpu.VMEM((ROWS, half * HD), jnp.bfloa...  76.4 us
    pallas_call x1, Pallas kernels, shards(): pl.pallas_call(finish_kernel, out_shape=(jax.ShapeDtypeStruct((ROWS, QH *...  2.06 us

profile of v4, /device:TPU:1, one launch (start us, length us, event | category | flops | bytes accessed | tf_op | source)
XLA Modules:
  0.0 79.1 jit_solution(6794280429394545838)
XLA Ops:
  0.6 76.4 %sync_and_attend.1 = (bf16[256,2048]{1,0:T(8,128)(2,1)S(1)}, bf16[16,256,256]{2,1,0:T(8,128)(2,1)S(1)}, bf16[256,256]{1,0:T(8,128)(2,1)S(1)}, f32[256,1024]{1,0:T(8,128)S(1)}, f32[256,1024]{1,0:T(8,128)S(1)}) custom-call(bf16[256,8192]{1,0:T(8,128)(2,1)} %bitcast.5, bf16[256,4096]{1,0:T(8,128)(2,1)} %bitcast.6, s32[1,256]{1,0:T(1,128)} %bitcast.9, ...), custom_call_target="tpu_custom_call" | custom-call | flops 6000000000 | bytes 13631488 | tf_op jit(solution)/shard_map/sync_and_attend/pallas_call | solution.py:370
  77.1 2.1 %finish.1 = (bf16[256,4096]{1,0:T(8,128)(2,1)}, f32[256,1024]{1,0:T(8,128)}, f32[256,1024]{1,0:T(8,128)}) custom-call(bf16[256,2048]{1,0:T(8,128)(2,1)S(1)} %get-tuple-element.11.mixed, bf16[16,256,256]{2,1,0:T(8,128)(2,1)S(1)} %get-tuple-element.12.late_probs, bf16[256,256]{1,0:T(8,128)(2,1)S(1)} %get-tuple-element.13.late_values, ...), custom_call_target="tpu_custom_call" | custom-call | tf_op jit(solution)/shard_map/finish/pallas_call | solution.py:404

commit v5 on v4

--- a/solution.py
+++ b/solution.py
@@ -30,14 +30,14 @@
     (1, 1): (0, 1), (-1, 1): (0, 1), (1, -1): (0, -1), (-1, -1): (0, -1), (0, 2): (0, 1),
     (2, 1): (-1, 1), (2, -1): (1, -1), (1, 2): (1, 1), (-1, 2): (-1, -1), (2, 2): (-1, 2),
 }
-TREES = (PARENTS | {(1, 2): (0, 2)}, PARENTS | {(-1, 2): (0, 2)}, PARENTS, PARENTS)
+TREES = (PARENTS | {(-1, 2): (0, 2)}, PARENTS | {(1, 2): (0, 2)}, PARENTS, PARENTS)
 ORDER = (
-    -33, -34, -2, -46, -18, -49, -16, -3, -47, -19, 1, -32, -4, 17, 15,
-    -17, -1, 7, 45, 2, 46, 19, 31, 3, 8, -31, 100, 51, 24, 16,
-    -48, 55, 0, 54, 28, 22, 20, 53, 37, 23, 21, 101, 13, 33, 6,
-    48, 4, 5, 38, 30, 9, 27, 29, 47, 26, 52, 25, 18, 14, 58,
-    50, 32, 11, 43, 35, 41, 12, 36, 10, 49, 39, 59, 56, 57, 42,
-    44, 40, 34, 102,
+    -18, -17, -49, -16, -2, -4, -48, -1, -34, -19, -31, -33, -3, 15, 32,
+    16, 0, 21, -47, 33, 23, 1, -32, 100, 17, 6, 22, 20, 34, 24,
+    -46, 18, 30, 8, 46, 28, 31, 2, 9, 26, 48, 25, 53, 19, 29,
+    27, 36, 5, 38, 45, 10, 13, 39, 7, 101, 40, 47, 58, 3, 52,
+    50, 37, 35, 12, 4, 51, 11, 14, 43, 54, 49, 56, 55, 57, 41,
+    59, 44, 42, 102,
 )
 GROUP = 4
 RECEIVES = [code for code in ORDER if 0 <= code < 100]
@@ -106,7 +106,7 @@
         source = weights.at[:, pl.ds(q * BLK, BLK)] if node == (0, 0) else gathered.at[at, q]
         return pltpu.make_async_remote_copy(
             src_ref=source, dst_ref=gathered.at[at, q],
-            send_sem=gsend.at[q, index], recv_sem=grecv.at[q, index],
+            send_sem=gsend, recv_sem=grecv.at[q, index],
             device_id=dev(*step_of(q, child)), device_id_type=MESH,
         )
 
@@ -119,7 +119,7 @@
         at, index = slot(node), NODES.index(node)
         pltpu.make_async_remote_copy(
             src_ref=gathered.at[at, q], dst_ref=gathered.at[at, q],
-            send_sem=gsend.at[q, index], recv_sem=grecv.at[q, index],
+            send_sem=gsend, recv_sem=grecv.at[q, index],
             device_id=sibling, device_id_type=MESH,
         ).wait_recv()
 
@@ -322,17 +322,18 @@
 
     for start in todo:
         softmax_heads(start)
-    for _, q in waiting:
-        settle(q)
-
-    for q in range(NQ):
-        for child in NODES:
-            hop(q, child).wait_send()
-        exchange(q).wait_send()
+    sent = gathered.at[pl.ds(0, CHIPS - 1)]
+    pltpu.make_async_remote_copy(
+        src_ref=sent, dst_ref=sent, send_sem=gsend, recv_sem=trecv, device_id=sibling, device_id_type=MESH
+    ).wait_send()
     all_feats(other).wait_send()
     for step in (1, 2, 3):
         raw_send(step).wait_send()
         spread(step).wait_send()
+    for _, q in waiting:
+        settle(q)
+    for q in range(NQ):
+        exchange(q).wait_send()
 
 
 def finish_kernel(
@@ -391,7 +392,7 @@
             pltpu.VMEM((PART, KVW), jnp.float32),
             pltpu.VMEM((PART, KVW), jnp.float32),
             pltpu.VMEM((X, PART, KVW), jnp.float32),
-            dma((NQ, 15)), dma((NQ, 15)), dma, dma, dma((3,)), dma((3,)), dma, dma, dma((3,)), dma((3,)),
+            dma, dma((NQ, 15)), dma, dma, dma((3,)), dma((3,)), dma, dma, dma((3,)), dma((3,)),
             dma((NQ,)), dma((NQ,)),
             dma((NQ,)), dma, dma, dma, dma, dma,
         ],

time: 79.2 us -> 78.5 us (level)
  no operation moved by 1% of the time
where the time goes in v5:
time: 78.5 us; the launch traced here: 78.4 us
  Pallas kernels  77.8 us (99%)
    pallas_call x1, Pallas kernels, shards(): pl.pallas_call(kernel, out_shape=(pltpu.VMEM((ROWS, half * HD), jnp.bfloa...  75.7 us
    pallas_call x1, Pallas kernels, shards(): pl.pallas_call(finish_kernel, out_shape=(jax.ShapeDtypeStruct((ROWS, QH *...  2.06 us

profile of v5, /device:TPU:1, one launch (start us, length us, event | category | flops | bytes accessed | tf_op | source)
XLA Modules:
  0.0 78.4 jit_solution(9392024014020643764)
XLA Ops:
  0.6 75.7 %sync_and_attend.1 = (bf16[256,2048]{1,0:T(8,128)(2,1)S(1)}, bf16[16,256,256]{2,1,0:T(8,128)(2,1)S(1)}, bf16[256,256]{1,0:T(8,128)(2,1)S(1)}, f32[256,1024]{1,0:T(8,128)S(1)}, f32[256,1024]{1,0:T(8,128)S(1)}) custom-call(bf16[256,8192]{1,0:T(8,128)(2,1)} %bitcast.5, bf16[256,4096]{1,0:T(8,128)(2,1)} %bitcast.6, s32[1,256]{1,0:T(1,128)} %bitcast.9, ...), custom_call_target="tpu_custom_call" | custom-call | flops 6000000000 | bytes 13631488 | tf_op jit(solution)/shard_map/sync_and_attend/pallas_call | solution.py:371
  76.4 2.1 %finish.1 = (bf16[256,4096]{1,0:T(8,128)(2,1)}, f32[256,1024]{1,0:T(8,128)}, f32[256,1024]{1,0:T(8,128)}) custom-call(bf16[256,2048]{1,0:T(8,128)(2,1)S(1)} %get-tuple-element.11.mixed, bf16[16,256,256]{2,1,0:T(8,128)(2,1)S(1)} %get-tuple-element.12.late_probs, bf16[256,256]{1,0:T(8,128)(2,1)S(1)} %get-tuple-element.13.late_values, ...), custom_call_target="tpu_custom_call" | custom-call | tf_op jit(solution)/shard_map/finish/pallas_call | solution.py:405

commit v6 on v5

--- a/solution.py
+++ b/solution.py
@@ -307,7 +307,7 @@
         if state["ready"] and (len(pending[q]) >= GROUP or left[q] == 0 or done > TAIL):
             flush(q)
         for item in list(waiting):
-            if done >= item[0] + 2 and (item[1] < 2 or not todo):
+            if done >= item[0] + 3 and (item[1] < 2 or not todo):
                 waiting.remove(item)
                 settle(item[1])
         if left[q] == 0:

time: 78.5 us -> 77.5 us (0.987)
  Pallas kernels: 77.8 us -> 76.7 us
    pallas_call x1, Pallas kernels: 75.7 us -> 74.7 us  [shards(): pl.pallas_call(kernel, out_shape=(pltpu.VMEM((ROWS, half * HD), jnp.bfloa...]
where the time goes in v6:
time: 77.5 us; the launch traced here: 77.4 us
  Pallas kernels  76.7 us (99%)
    pallas_call x1, Pallas kernels, shards(): pl.pallas_call(kernel, out_shape=(pltpu.VMEM((ROWS, half * HD), jnp.bfloa...  74.7 us
    pallas_call x1, Pallas kernels, shards(): pl.pallas_call(finish_kernel, out_shape=(jax.ShapeDtypeStruct((ROWS, QH *...  2.06 us

profile of v6, /device:TPU:1, one launch (start us, length us, event | category | flops | bytes accessed | tf_op | source)
XLA Modules:
  0.0 77.4 jit_solution(10189424621189154761)
XLA Ops:
  0.6 74.7 %sync_and_attend.1 = (bf16[256,2048]{1,0:T(8,128)(2,1)S(1)}, bf16[16,256,256]{2,1,0:T(8,128)(2,1)S(1)}, bf16[256,256]{1,0:T(8,128)(2,1)S(1)}, f32[256,1024]{1,0:T(8,128)S(1)}, f32[256,1024]{1,0:T(8,128)S(1)}) custom-call(bf16[256,8192]{1,0:T(8,128)(2,1)} %bitcast.5, bf16[256,4096]{1,0:T(8,128)(2,1)} %bitcast.6, s32[1,256]{1,0:T(1,128)} %bitcast.9, ...), custom_call_target="tpu_custom_call" | custom-call | flops 6000000000 | bytes 13631488 | tf_op jit(solution)/shard_map/sync_and_attend/pallas_call | solution.py:371
  75.3 2.1 %finish.1 = (bf16[256,4096]{1,0:T(8,128)(2,1)}, f32[256,1024]{1,0:T(8,128)}, f32[256,1024]{1,0:T(8,128)}) custom-call(bf16[256,2048]{1,0:T(8,128)(2,1)S(1)} %get-tuple-element.11.mixed, bf16[16,256,256]{2,1,0:T(8,128)(2,1)S(1)} %get-tuple-element.12.late_probs, bf16[256,256]{1,0:T(8,128)(2,1)S(1)} %get-tuple-element.13.late_values, ...), custom_call_target="tpu_custom_call" | custom-call | tf_op jit(solution)/shard_map/finish/pallas_call | solution.py:405
